TPU v7x, 32 devices: a whole 2x2x4 slice. The times are simulated.
32 devices in a mesh: groups: 2 (over y), seq: 16 (over z, x, core).
Axes of the slice: x: 2, y: 2, z: 4, core: 2. Of those that a mesh axis runs over, the one named last changes fastest.
Arguments:
- queries: bfloat16 [8192, 2048], P(('groups', 'seq')), parts along dimension 0, may hold values from -6 to 6
- key_inputs: bfloat16 [8192, 2048], P(('groups', 'seq')), parts along dimension 0, may hold values from -6 to 6
- values: bfloat16 [8192, 2048], P(('groups', 'seq')), parts along dimension 0, may hold values from -6 to 6
- short_taps: float32 [3, 3, 2048], replicated, may hold values from -3.6 to 3.6
- decay_rates: float32 [2, 2048], replicated, may hold values from 2.4414063e-05 to 0.05, as said below
- residues: float32 [2, 2048], replicated, may hold values from -6 to 6
- skip_gain: float32 [2048], replicated, may hold values from -6 to 6
- out_weight: bfloat16 [2048, 4096], P('seq'), may hold values from -0.125 to 0.125
- cotangent: bfloat16 [8192, 4096], P(('groups', 'seq')), parts along dimension 0, may hold values from -6 to 6
- doc_blocks: int32 [8], P('groups'), parts along dimension 0, may hold values from 1 to 16, 32 in all
Outputs:
- mixed_out: bfloat16 [8192, 4096], P(('groups', 'seq')), parts along dimension 0
- grad_queries: bfloat16 [8192, 2048], P(('groups', 'seq')), parts along dimension 0
- grad_keys: bfloat16 [8192, 2048], P(('groups', 'seq')), parts along dimension 0
- grad_values: bfloat16 [8192, 2048], P(('groups', 'seq')), parts along dimension 0
There are 2 independent parts, one for each index of `groups`. A program takes and returns all parts, laid end to end along the dimension named above; an argument that names none is the same for every part. Nothing has to cross between parts.
Inputs may be any that keep to these rules, and one draw needn't show every extreme that they name: `doc_blocks`: documents fill the batch in order: the entries sum to 32, and the longest is exactly 16 blocks. `decay_rates`: positive decay rates.
All inputs are finite; a program needn't handle non-finite values.
Results may differ from a plain program's by a relative error of at most 0.0051.
Values may be sent and summed in bfloat16 or wider, within the bound.
A program may use at most 128 MiB of HBM per device.

v0:
```python
import jax
import jax.numpy as jnp
from jax import lax
from jax.sharding import PartitionSpec as P

BLOCK = 128
exact_mode = lax.Precision.HIGHEST


def from_behind(value, axis, steps):
    count = lax.axis_size(axis)
    leading, last = (max(0, -steps), min(count, count - steps))
    return lax.ppermute(value, axis, [(source, source + steps) for source in range(leading, last)])


def combine(earlier, later):
    return (earlier[0] * later[0], later[0] * earlier[1] + later[1])


def block_marks(doc_blocks, first_block, block_count):
    doc_ends = jnp.cumsum(doc_blocks)
    starts = doc_ends - doc_blocks
    block_index = first_block + jnp.arange(block_count, dtype=jnp.int32)
    matches = (block_index[:, None] == starts[None, :]) | (block_index[:, None] >= doc_ends[-1])
    return jnp.any(matches, axis=1).astype(jnp.float32)


def block_parts(blocked, decay_rates, reset_flags):
    span = blocked.shape[-1]
    offsets = jnp.arange(span, dtype=jnp.float32)
    upper_ones = (offsets[:, None] <= offsets[None, :]).astype(jnp.float32)
    growth = jnp.exp(decay_rates[:, :, None] * offsets[None, None, :])
    shrink = jnp.exp(-decay_rates[:, :, None] * offsets[None, None, :])
    lifted = blocked[None, :, :, :] * growth[:, :, None, :]
    inside = (
        jnp.einsum("sgbp,pt->sgbt", lifted, upper_ones, precision=exact_mode)
        * shrink[:, :, None, :]
    )
    keep_rate = (1.0 - reset_flags)[None, None, :] * jnp.exp(-decay_rates * span)[:, :, None]
    cum_keep, cum_ends = lax.associative_scan(combine, (keep_rate, inside[..., -1]), axis=2)
    return (inside, cum_keep, cum_ends)


def block_finish(inside, cum_keep, cum_ends, decay_rates, filter_weight, reset_flags, incoming):
    span = inside.shape[-1]
    at_end = cum_keep * incoming[:, :, None] + cum_ends
    before = (
        jnp.concatenate([incoming[:, :, None], at_end[:, :, :-1]], axis=2)
        * (1.0 - reset_flags)[None, None, :]
    )
    offsets = jnp.arange(1, span + 1, dtype=jnp.float32)
    decay_rows = jnp.exp(-decay_rates[:, :, None] * offsets[None, None, :])
    summed_up = inside + before[..., None] * decay_rows[:, :, None, :]
    return jnp.sum(summed_up * filter_weight[:, :, None, None], axis=0)


def relay_pass(columns, decay_rates, filter_weight, doc_blocks, backward):
    device_place = lax.axis_index("seq")
    spread = lax.all_to_all(columns, "seq", split_axis=0, concat_axis=1, tiled=True)
    share_width = spread.shape[0]
    block_count = spread.shape[1] // BLOCK
    own_rates = lax.dynamic_slice_in_dim(decay_rates, device_place * share_width, share_width, 1)
    own_weights = lax.dynamic_slice_in_dim(
        filter_weight, device_place * share_width, share_width, 1
    )
    lead_shift = 1 if backward else 0
    reset_flags = block_marks(doc_blocks, lead_shift, block_count)
    blocked = spread.reshape(share_width, block_count, BLOCK)
    if backward:
        blocked = jnp.flip(blocked, axis=(1, 2))
        reset_flags = jnp.flip(reset_flags, axis=0)
    inside, cum_keep, cum_ends = block_parts(blocked, own_rates, reset_flags)
    zero_state = jnp.zeros(own_rates.shape, jnp.float32)
    result = block_finish(
        inside, cum_keep, cum_ends, own_rates, own_weights, reset_flags, zero_state
    )
    if backward:
        result = jnp.flip(result, axis=(1, 2))
    return lax.all_to_all(
        result.reshape(share_width, block_count * BLOCK),
        "seq",
        split_axis=1,
        concat_axis=0,
        tiled=True,
    )


def long_conv(columns, decay_rates, filter_weight, doc_blocks, backward):
    return relay_pass(columns, decay_rates, filter_weight, doc_blocks, backward)


def on_device(
    queries,
    key_inputs,
    values,
    short_taps,
    decay_rates,
    residues,
    skip_gain,
    out_weight,
    cotangent,
    doc_blocks,
):
    row_count = queries.shape[0]
    block_count = row_count // BLOCK
    marks_ext = block_marks(doc_blocks, lax.axis_index("seq") * block_count, block_count + 1)
    head_mask = (jnp.arange(BLOCK) == 0).astype(jnp.float32)
    begins = (marks_ext[:, None] * head_mask[None, :]).reshape(-1)[: row_count + 2]
    now_start = begins[:row_count]
    prior_start = jnp.concatenate([jnp.zeros((1,), jnp.float32), now_start[:-1]])
    keep_one = (1.0 - now_start)[:, None]
    keep_two = keep_one * (1.0 - prior_start)[:, None]
    next_one = (1.0 - begins[1 : row_count + 1])[:, None]
    next_two = next_one * (1.0 - begins[2 : row_count + 2])[:, None]
    tail_rows = jnp.stack(
        [queries[row_count - 2 :], key_inputs[row_count - 2 :], values[row_count - 2 :]]
    )
    prev_rims = from_behind(tail_rows, "seq", 1)

    def forward_short(current, rim_rows, tap_row):
        longer = jnp.concatenate([rim_rows, current], axis=0).astype(jnp.float32)
        return (
            tap_row[0] * longer[2:]
            + tap_row[1] * keep_one * longer[1:-1]
            + tap_row[2] * keep_two * longer[:-2]
        )

    q_short = forward_short(queries, prev_rims[0], short_taps[0])
    k_short = forward_short(key_inputs, prev_rims[1], short_taps[1])
    v_short = forward_short(values, prev_rims[2], short_taps[2])
    product = k_short * v_short
    filter_weight = residues * jnp.sqrt(2.0 * decay_rates)
    conv_out = (
        long_conv(product.T, decay_rates, filter_weight, doc_blocks, False).T + skip_gain * product
    )
    gated_rows = (q_short * conv_out).astype(jnp.bfloat16)
    weight_piece = lax.all_gather(out_weight, "seq", axis=0, tiled=True)
    total_out = jnp.dot(gated_rows, weight_piece, preferred_element_type=jnp.float32)
    column = lax.dot_general(
        cotangent, weight_piece, (((1,), (1,)), ((), ())), preferred_element_type=jnp.float32
    )
    total_out, grad_gated = (total_out, column)
    mixed_out = total_out.astype(jnp.bfloat16)
    grad_qs = grad_gated * conv_out
    grad_conv = grad_gated * q_short
    grad_product = (
        long_conv(grad_conv.T, decay_rates, filter_weight, doc_blocks, True).T
        + skip_gain * grad_conv
    )
    grad_ks = grad_product * v_short
    grad_vs = grad_product * k_short
    head_rows = jnp.stack([grad_qs[:2], grad_ks[:2], grad_vs[:2]])
    next_rims = from_behind(head_rows.astype(jnp.bfloat16), "seq", -1).astype(head_rows.dtype)

    def backward_short(gradient, rim_rows, tap_row):
        longer = jnp.concatenate([gradient, rim_rows], axis=0)
        summed = (
            tap_row[0] * gradient
            + tap_row[1] * next_one * longer[1 : row_count + 1]
            + tap_row[2] * next_two * longer[2:]
        )
        return summed.astype(jnp.bfloat16)

    grad_queries = backward_short(grad_qs, next_rims[0], short_taps[0])
    grad_keys = backward_short(grad_ks, next_rims[1], short_taps[1])
    grad_values = backward_short(grad_vs, next_rims[2], short_taps[2])
    return (mixed_out, grad_queries, grad_keys, grad_values)


def solution(mesh):
    return jax.shard_map(
        on_device,
        mesh=mesh,
        in_specs=(
            P(("groups", "seq"), None),
            P(("groups", "seq"), None),
            P(("groups", "seq"), None),
            P(),
            P(),
            P(),
            P(),
            P("seq", None),
            P(("groups", "seq"), None),
            P("groups"),
        ),
        out_specs=(
            P(("groups", "seq"), None),
            P(("groups", "seq"), None),
            P(("groups", "seq"), None),
            P(("groups", "seq"), None),
        ),
        check_vma=False,
    )
```

profile of v0, /device:TPU:16, one launch (start us, length us, event | category | flops | bytes accessed | tf_op | source)
XLA Modules:
  0.0 414.4 jit_solution(16186817507365080882)
XLA Ops:
  7.2 0.7 all-gather.2.cloned.1.call-update
  7.9 0.8 slice_bitcast_fusion.8
  8.7 0.8 slice_bitcast_fusion.6
  9.6 1.9 collective-permute-start
  11.5 0.8 reduce-window.4
  12.9 0.7 broadcast_compare_fusion.1
  13.6 0.7 bitcast_subtract_fusion
  14.5 0.7 fusion.63
  15.2 1.6 fusion.71
  16.9 0.6 slice_bitcast_fusion.4
  18.2 3.1 multiply_bitcast_fusion.1
  21.4 1.5 copy.42
  22.9 6.6 %all-to-all-start = ((f32[16,128,256]{1,2,0:T(8,128)}), f32[16,128,256]{1,2,0:T(8,128)}, u32[]{:S(2)}, u32[]{:S(2)}) async-start(f32[16,128,256]{1,2,0:T(8,128)} %bitcast.121), calls=%async_computation | async-start | bytes 4194304 | tf_op jit(solution)/shard_map/all_to_all | solution.py:59
  29.5 0.7 iota_compare_fusion.2
  30.3 1.3 dynamic-slice_multiply_fusion
  32.9 0.6 slice.510
  33.5 0.6 slice.491
  34.1 0.6 slice.490
  35.3 0.6 slice.558
  35.9 0.6 slice.539
  36.5 0.6 slice.538
  37.2 0.8 multiply_exponential_fusion
  38.0 2.5 maximum_convert_fusion
  40.5 68.7 %all-to-all-done = f32[16,128,256]{1,2,0:T(8,128)} async-done(((f32[16,128,256]{1,2,0:T(8,128)}), f32[16,128,256]{1,2,0:T(8,128)}, u32[]{:S(2)}, u32[]{:S(2)}) %all-to-all-start) | async-done | bytes 2097184 | tf_op jit(solution)/shard_map/all_to_all | solution.py:59
  109.2 2.9 copy.23
  112.2 60.0 %all-gather.2.cloned.1.call-done = bf16[2048,4096]{1,0:T(8,128)(2,1)} async-done(((bf16[128,4096]{1,0:T(8,128)(2,1)}), bf16[2048,4096]{1,0:T(8,128)(2,1)}) %all-gather.2.cloned.1.call-update) | async-done | bytes 16777232 | tf_op jit(solution)/shard_map/all_gather | solution.py:137
  172.2 9.5 %fusion.82 = f32[256,2048]{1,0:T(8,128)} fusion(bf16[256,4096]{1,0:T(8,128)(2,1)S(1)} %copy-done, bf16[2048,4096]{1,0:T(8,128)(2,1)} %all-gather.2.cloned.1.call-done), kind=kOutput, calls=%fused_computation.202 | convolution fusion | flops 4294967296 | bytes 20971520 | tf_op jit(solution)/shard_map/dot_general | solution.py:139
  181.7 6.8 %multiply_bitcast_fusion = (f32[32,16,8,128]{3,2,1,0:T(8,128)S(1)}, f32[256,2048]{1,0:T(8,128)}) fusion(f32[256,2048]{1,0:T(8,128)} %fusion.82, f32[258,2048]{1,0:T(8,128)} %maximum_convert_fusion, f32[256]{0:T(256)S(1)} %copy-done.30, f32[2048]{0:T(1024)S(1)} %bitcast.143, f32[256]{0:T(256)S(1)} %copy-done.28, f32[2048]{0:T(1024)S(1)} %bitcast.145, ...), kind=kLoop, calls=%fused_computation.65 | loop fusion | flops 4194304 | bytes 12609536
  188.4 1.5 copy.41
  190.0 6.7 %all-to-all-start.2 = ((f32[16,128,256]{1,2,0:T(8,128)}), f32[16,128,256]{1,2,0:T(8,128)}, u32[]{:S(2)}, u32[]{:S(2)}) async-start(f32[16,128,256]{1,2,0:T(8,128)} %bitcast.120), calls=%async_computation.2 | async-start | bytes 4194304 | tf_op jit(solution)/shard_map/all_to_all | solution.py:59
  196.7 2.8 fusion.4
  199.6 2.0 copy-done.4
  202.9 41.5 %all-to-all-done.2 = f32[16,128,256]{1,2,0:T(8,128)} async-done(((f32[16,128,256]{1,2,0:T(8,128)}), f32[16,128,256]{1,2,0:T(8,128)}, u32[]{:S(2)}, u32[]{:S(2)}) %all-to-all-start.2) | async-done | bytes 2097184 | tf_op jit(solution)/shard_map/all_to_all | solution.py:59
  244.4 16.5 %rev.11 = f32[128,32,128]{0,2,1:T(8,128)} reverse(f32[128,32,128]{0,2,1:T(8,128)} %bitcast.32), dimensions={1,2} | reverse | bytes 4194304 | tf_op jit(solution)/shard_map/jit(_flip)/rev | solution.py:70
  260.9 1.9 copy.27
  262.9 2.8 fusion.7
  265.8 2.0 copy-done.5
  269.1 6.8 %multiply_reduce_fusion = (f32[128,32,128]{0,2,1:T(8,128)S(1)}, f32[128,32,128]{0,2,1:T(8,128)}) fusion(f32[2,128,32,128]{1,3,2,0:T(8,128)} %copy-done.5, f32[2,128,32]{1,2,0:T(8,128)S(1)} %pad_multiply_fusion, f32[2,128]{1,0:T(2,128)S(1)} %copy-done.33, f32[2,128,128]{1,2,0:T(8,128)S(1)} %get-tuple-element.90, f32[2,128,32,128]{1,3,2,0:T(8,128)} %copy-done.4, ...), kind=kLoop, calls=%fused_computation.1 | loop fusion | flops 7340032 | bytes 12780544 | tf_op jit(solution)/shard_map/reduce_sum | solution.py:54
  275.9 4.7 %all-to-all-start.1 = ((f32[128,16,256]{0,2,1:T(8,128)}), f32[128,16,256]{0,2,1:T(8,128)}, u32[]{:S(2)}, u32[]{:S(2)}) async-start(f32[128,16,256]{0,2,1:T(8,128)} %bitcast.119), calls=%async_computation.1 | async-start | bytes 4194304 | tf_op jit(solution)/shard_map/all_to_all | solution.py:79
  280.6 10.3 %rev.13 = f32[128,32,128]{0,2,1:T(8,128)} reverse(f32[128,32,128]{0,2,1:T(8,128)S(1)} %get-tuple-element.4), dimensions={1,2} | reverse | bytes 4194304 | tf_op jit(solution)/shard_map/jit(_flip)/rev | solution.py:78
  290.9 37.5 %all-to-all-done.1 = f32[128,16,256]{0,2,1:T(8,128)} async-done(((f32[128,16,256]{0,2,1:T(8,128)}), f32[128,16,256]{0,2,1:T(8,128)}, u32[]{:S(2)}, u32[]{:S(2)}) %all-to-all-start.1) | async-done | bytes 2097184 | tf_op jit(solution)/shard_map/all_to_all | solution.py:79
  328.4 4.8 %all-to-all-start.3 = ((f32[128,16,256]{0,2,1:T(8,128)}), f32[128,16,256]{0,2,1:T(8,128)}, u32[]{:S(2)}, u32[]{:S(2)}) async-start(f32[128,16,256]{0,2,1:T(8,128)} %bitcast.122), calls=%async_computation.3 | async-start | bytes 4194304 | tf_op jit(solution)/shard_map/all_to_all | solution.py:79
  333.3 47.7 %all-to-all-done.3 = f32[128,16,256]{0,2,1:T(8,128)} async-done(((f32[128,16,256]{0,2,1:T(8,128)}), f32[128,16,256]{0,2,1:T(8,128)}, u32[]{:S(2)}, u32[]{:S(2)}) %all-to-all-start.3) | async-done | bytes 2097184 | tf_op jit(solution)/shard_map/all_to_all | solution.py:79
  380.9 5.2 %fusion.64 = (f32[256,2048]{1,0:T(8,128)S(1)}, f32[256,2048]{1,0:T(8,128)S(1)}, f32[256,2048]{1,0:T(8,128)S(1)}, f32[256,2048]{1,0:T(8,128)S(1)}) fusion(f32[256,2048]{1,0:T(8,128)} %get-tuple-element.13, f32[256,2048]{1,0:T(8,128)} %fusion.82, f32[256,2048]{1,0:T(8,128)} %get-tuple-element.18, f32[2048]{0:T(1024)S(1)} %copy-done.31, ...), kind=kLoop, calls=%fused_computation.189 | loop fusion | flops 4194304 | bytes 20979712 | tf_op jit(solution)/shard_map/mul | solution.py:150
  386.6 3.2 collective-permute-start.1
  389.8 11.6 %convolution_convert_fusion = bf16[256,4096]{1,0:T(8,128)(2,1)} fusion(bf16[2048,4096]{1,0:T(8,128)(2,1)} %all-gather.2.cloned.1.call-done, f32[256,2048]{1,0:T(8,128)S(1)} %copy-done.6, f32[256,2048]{1,0:T(8,128)S(1)} %get-tuple-element.20), kind=kOutput, calls=%fused_computation | convolution fusion | flops 4297064448 | bytes 23068672 | tf_op jit(solution)/shard_map/dot_general | solution.py:138
  401.5 1.9 fusion.24
  403.4 4.2 %fusion.14 = (bf16[256,2048]{1,0:T(8,128)(2,1)}, bf16[256,2048]{1,0:T(8,128)(2,1)}) fusion(f32[256,2048]{1,0:T(8,128)S(1)} %mul.732, f32[2,2048]{1,0:T(2,128)S(1)} %get-tuple-element.30, f32[256]{0:T(256)S(1)} %get-tuple-element.71, f32[256]{0:T(256)S(1)} %get-tuple-element.70, f32[2048]{0:T(1024)S(1)} %bitcast.140, f32[2048]{0:T(1024)S(1)} %bitcast.142, ...), kind=kLoop, calls=%fused_computation.19 | loop fusion | flops 10485760 | bytes 6375424 | tf_op jit(solution)/shard_map/convert_element_type | solution.py:162
  (247 shorter events, 6.3 us)
Async XLA Ops:
  7.2 165.0 %copy-start = (bf16[256,4096]{1,0:T(8,128)(2,1)S(1)}, bf16[256,4096]{1,0:T(8,128)(2,1)}, u32[]{:S(2)}) copy-start(bf16[256,4096]{1,0:T(8,128)(2,1)} %param.18) | copy-start | bytes 6291460
  7.2 10.4 %copy-start.7 = (bf16[256,2048]{1,0:T(8,128)(2,1)S(1)}, bf16[256,2048]{1,0:T(8,128)(2,1)}, u32[]{:S(2)}) copy-start(bf16[256,2048]{1,0:T(8,128)(2,1)} %param.11) | copy-start | bytes 3145732
  7.2 165.0 %all-gather.2.cloned.1.call-start = ((), (), s32[]{:S(2)}) async-start(), calls=%async_computation.4 | async-start | bytes 17825792 | tf_op jit(solution)/shard_map/all_gather | solution.py:137
  9.6 7.4 %collective-permute-start = (bf16[3,2,2048]{2,1,0:T(2,128)(2,1)S(1)}, bf16[3,2,2048]{2,1,0:T(2,128)(2,1)S(1)}, u32[]{:S(2)}, u32[]{:S(2)}) collective-permute-start(bf16[3,2,2048]{2,1,0:T(2,128)(2,1)S(1)} %pad_maximum_fusion.3), channel_id=1, source_target_pairs={{0,1},{1,2},{2,3},{3,4},{4,5},{5,6},{6,7},{7,8},{8,9},{9,10},{10,1... | collective-permute-start | bytes 73736 | tf_op jit(solution)/shard_map/ppermute | solution.py:13
  12.9 4.9 %copy-start.8 = (bf16[256,2048]{1,0:T(8,128)(2,1)S(1)}, bf16[256,2048]{1,0:T(8,128)(2,1)}, u32[]{:S(2)}) copy-start(bf16[256,2048]{1,0:T(8,128)(2,1)} %param.12) | copy-start | bytes 3145732
  16.8 1.4 copy-start.10
  16.8 1.4 copy-start.12
  16.8 1.4 copy-start.14
  16.8 1.4 copy-start.16
  16.9 1.3 copy-start.27
  16.9 1.3 copy-start.29
  22.9 15.1 %copy-start.9 = (bf16[256,2048]{1,0:T(8,128)(2,1)S(1)}, bf16[256,2048]{1,0:T(8,128)(2,1)}, u32[]{:S(2)}) copy-start(bf16[256,2048]{1,0:T(8,128)(2,1)} %param.10) | copy-start | bytes 3145732
  22.9 86.3 %all-to-all-start = ((f32[16,128,256]{1,2,0:T(8,128)}), f32[16,128,256]{1,2,0:T(8,128)}, u32[]{:S(2)}, u32[]{:S(2)}) async-start(f32[16,128,256]{1,2,0:T(8,128)} %bitcast.121), calls=%async_computation | async-start | bytes 4194304 | tf_op jit(solution)/shard_map/all_to_all | solution.py:59
  31.6 5.5 %copy-start.36 = (f32[32]{0:T(128)}, f32[32]{0:T(128)S(1)}, u32[]{:S(2)}) copy-start(f32[32]{0:T(128)S(1)} %broadcast_subtract_fusion.1) | copy-start | bytes 388
  31.6 5.5 %copy-start.38 = (f32[32]{0:T(128)}, f32[32]{0:T(128)S(1)}, u32[]{:S(2)}) copy-start(f32[32]{0:T(128)S(1)} %convert_subtract_fusion) | copy-start | bytes 388
  112.1 69.5 %copy-start.18 = (f32[1,1,2048]{2,1,0:T(1,128)S(1)}, f32[1,1,2048]{2,1,0:T(1,128)}, u32[]{:S(2)}) copy-start(f32[1,1,2048]{2,1,0:T(1,128)} %get-tuple-element.25) | copy-start | bytes 24580
  112.1 69.5 %copy-start.19 = (f32[1,1,2048]{2,1,0:T(1,128)S(1)}, f32[1,1,2048]{2,1,0:T(1,128)}, u32[]{:S(2)}) copy-start(f32[1,1,2048]{2,1,0:T(1,128)} %get-tuple-element.26) | copy-start | bytes 24580
  112.1 69.5 %copy-start.20 = (f32[1,1,2048]{2,1,0:T(1,128)S(1)}, f32[1,1,2048]{2,1,0:T(1,128)}, u32[]{:S(2)}) copy-start(f32[1,1,2048]{2,1,0:T(1,128)} %get-tuple-element.27) | copy-start | bytes 24580
  112.1 69.5 %copy-start.28 = (f32[256]{0:T(256)S(1)}, f32[256]{0:T(256)}, u32[]{:S(2)}) copy-start(f32[256]{0:T(256)} %copy-done.27) | copy-start | bytes 3076
  112.1 69.5 %copy-start.30 = (f32[256]{0:T(256)S(1)}, f32[256]{0:T(256)}, u32[]{:S(2)}) copy-start(f32[256]{0:T(256)} %copy-done.29) | copy-start | bytes 3076
  190.0 6.7 %copy-start.2 = (f32[128,32,128]{2,0,1:T(8,128)S(1)}, f32[128,32,128]{2,0,1:T(8,128)}, u32[]{:S(2)}) copy-start(f32[128,32,128]{2,0,1:T(8,128)} %copy.23) | copy-start | bytes 6291460
  190.0 54.5 %all-to-all-start.2 = ((f32[16,128,256]{1,2,0:T(8,128)}), f32[16,128,256]{1,2,0:T(8,128)}, u32[]{:S(2)}, u32[]{:S(2)}) async-start(f32[16,128,256]{1,2,0:T(8,128)} %bitcast.120), calls=%async_computation.2 | async-start | bytes 4194304 | tf_op jit(solution)/shard_map/all_to_all | solution.py:59
  196.7 5.0 %copy-start.23 = (f32[2,128,16]{1,2,0:T(8,128)S(1)}, f32[2,128,16]{1,2,0:T(8,128)}, u32[]{:S(2)}) copy-start(f32[2,128,16]{1,2,0:T(8,128)} %slice.491) | copy-start | bytes 49156
  196.7 5.0 %copy-start.24 = (f32[2,128,16]{1,2,0:T(8,128)S(1)}, f32[2,128,16]{1,2,0:T(8,128)}, u32[]{:S(2)}) copy-start(f32[2,128,16]{1,2,0:T(8,128)} %slice.490) | copy-start | bytes 49156
  196.7 6.0 %copy-start.26 = (f32[2,128,15]{1,2,0:T(8,128)S(1)}, f32[2,128,15]{1,2,0:T(8,128)}, u32[]{:S(2)}) copy-start(f32[2,128,15]{1,2,0:T(8,128)} %slice.510) | copy-start | bytes 46084
  196.7 6.0 %copy-start.35 = (f32[2,128,1]{1,2,0:T(1,128)S(1)}, f32[2,128,1]{1,2,0:T(1,128)}, u32[]{:S(2)}) copy-start(f32[2,128,1]{1,2,0:T(1,128)} %slice.607) | copy-start | bytes 3076
  196.7 6.2 %copy-start.39 = (f32[32]{0:T(128)S(1)}, f32[32]{0:T(128)}, u32[]{:S(2)}) copy-start(f32[32]{0:T(128)} %copy-done.38) | copy-start | bytes 388
  199.5 2.1 copy-start.4
  262.9 5.0 %copy-start.21 = (f32[2,128,16]{1,2,0:T(8,128)S(1)}, f32[2,128,16]{1,2,0:T(8,128)}, u32[]{:S(2)}) copy-start(f32[2,128,16]{1,2,0:T(8,128)} %slice.539) | copy-start | bytes 49156
  262.9 5.0 %copy-start.22 = (f32[2,128,16]{1,2,0:T(8,128)S(1)}, f32[2,128,16]{1,2,0:T(8,128)}, u32[]{:S(2)}) copy-start(f32[2,128,16]{1,2,0:T(8,128)} %slice.538) | copy-start | bytes 49156
  262.9 6.0 %copy-start.25 = (f32[2,128,15]{1,2,0:T(8,128)S(1)}, f32[2,128,15]{1,2,0:T(8,128)}, u32[]{:S(2)}) copy-start(f32[2,128,15]{1,2,0:T(8,128)} %slice.558) | copy-start | bytes 46084
  262.9 6.0 %copy-start.34 = (f32[2,128,1]{1,2,0:T(1,128)S(1)}, f32[2,128,1]{1,2,0:T(1,128)}, u32[]{:S(2)}) copy-start(f32[2,128,1]{1,2,0:T(1,128)} %slice.639) | copy-start | bytes 3076
  262.9 6.1 %copy-start.37 = (f32[32]{0:T(128)S(1)}, f32[32]{0:T(128)}, u32[]{:S(2)}) copy-start(f32[32]{0:T(128)} %copy-done.36) | copy-start | bytes 388
  262.9 6.2 %copy-start.33 = (f32[2,128]{1,0:T(2,128)S(1)}, f32[2,128]{1,0:T(2,128)}, u32[]{:S(2)}) copy-start(f32[2,128]{1,0:T(2,128)} %get-tuple-element.15) | copy-start | bytes 3076
  265.8 2.0 copy-start.5
  275.9 52.4 %all-to-all-start.1 = ((f32[128,16,256]{0,2,1:T(8,128)}), f32[128,16,256]{0,2,1:T(8,128)}, u32[]{:S(2)}, u32[]{:S(2)}) async-start(f32[128,16,256]{0,2,1:T(8,128)} %bitcast.119), calls=%async_computation.1 | async-start | bytes 4194304 | tf_op jit(solution)/shard_map/all_to_all | solution.py:79
  328.4 4.8 %copy-start.32 = (f32[384]{0:T(512)S(1)}, f32[384]{0:T(512)}, u32[]{:S(2)}) copy-start(f32[384]{0:T(512)} %get-tuple-element.86) | copy-start | bytes 4612
  328.4 52.6 %copy-start.3 = (f32[256,2048]{1,0:T(8,128)S(1)}, f32[256,2048]{1,0:T(8,128)}, u32[]{:S(2)}) copy-start(f32[256,2048]{1,0:T(8,128)} %get-tuple-element.14) | copy-start | bytes 6291460
  328.4 52.6 %copy-start.31 = (f32[2048]{0:T(1024)S(1)}, f32[2048]{0:T(1024)}, u32[]{:S(2)}) copy-start(f32[2048]{0:T(1024)} %param.16) | copy-start | bytes 24580
  328.4 52.6 %all-to-all-start.3 = ((f32[128,16,256]{0,2,1:T(8,128)}), f32[128,16,256]{0,2,1:T(8,128)}, u32[]{:S(2)}, u32[]{:S(2)}) async-start(f32[128,16,256]{0,2,1:T(8,128)} %bitcast.122), calls=%async_computation.3 | async-start | bytes 4194304 | tf_op jit(solution)/shard_map/all_to_all | solution.py:79
  386.2 3.6 copy-start.6
  386.6 14.8 %collective-permute-start.1 = (bf16[3,2,2048]{2,1,0:T(2,128)(2,1)S(1)}, bf16[3,2,2048]{2,1,0:T(2,128)(2,1)S(1)}, u32[]{:S(2)}, u32[]{:S(2)}) collective-permute-start(bf16[3,2,2048]{2,1,0:T(2,128)(2,1)S(1)} %pad_maximum_fusion.4), channel_id=1, source_target_pairs={{1,0},{2,1},{3,2},{4,3},{5,4},{6,5},{7,6},{8,7},{9,8},{10,9},{11,1... | collective-permute-start | bytes 73736 | tf_op jit(solution)/shard_map/ppermute | solution.py:13
  401.4 2.0 copy-start.11
  401.4 2.0 copy-start.13
  401.4 2.0 copy-start.15
  401.4 2.0 copy-start.17
  403.4 4.2 %copy-start.1 = (bf16[256,4096]{1,0:T(8,128)(2,1)S(1)}, bf16[256,4096]{1,0:T(8,128)(2,1)}, u32[]{:S(2)}) copy-start(bf16[256,4096]{1,0:T(8,128)(2,1)} %param.18) | copy-start | bytes 6291460
Sparse Core Ops, SparseCore 0:
  10.2 161.9 all-gather.1
where the time goes:
time: 416 us; the launch traced here: 414 us
  waiting for transfers between devices  256 us (62%)
  local copies, waits for them, and re-layouts  49.7 us (12%)
  other arithmetic  38.9 us (9%)
  starting transfers between devices  28 us (7%)
  matrix products  26.6 us (6%)
  between operations  15.2 us (4%)
    all_to_all x2, waiting for transfers between devices, relay_pass(): lax.all_to_all(columns, 'seq', split_axis=0, concat_axis=1, tiled=True)  110 us
    all_to_all x2, waiting for transfers between devices, relay_pass(): lax.all_to_all(result.reshape(share_width, block_count * BLOCK), 'seq', s...  85.2 us
    all_gather x1, waiting for transfers between devices, on_device(): weight_piece = lax.all_gather(out_weight, 'seq', axis=0, tiled=True)  60 us
    rev x2, local copies, waits for them, and re-layouts, relay_pass(): blocked = jnp.flip(blocked, axis=(1, 2))  18.5 us
    all_to_all x2, starting transfers between devices, relay_pass(): lax.all_to_all(columns, 'seq', split_axis=0, concat_axis=1, tiled=True)  13.3 us
    dot_general x1, matrix products, on_device(): jnp.dot(gated_rows, weight_piece, preferred_element_type=jnp.float32)  11.6 us
    rev x1, local copies, waits for them, and re-layouts, relay_pass(): result = jnp.flip(result, axis=(1, 2))  10.3 us
    unnamed x2, other arithmetic  9.89 us
  transfers between devices with their start and end apart: 7, of which 5 were waited for; matrix products, arithmetic and copies ran while one was open for 13% of the time, Pallas kernels for 0%

commit v1 on v0

--- a/solution.py
+++ b/solution.py
@@ -134,7 +134,21 @@
         long_conv(product.T, decay_rates, filter_weight, doc_blocks, False).T + skip_gain * product
     )
     gated_rows = (q_short * conv_out).astype(jnp.bfloat16)
-    weight_piece = lax.all_gather(out_weight, "seq", axis=0, tiled=True)
+    finding, u1, view_out = (
+        jax.lax.axis_size("seq"),
+        jax.lax.axis_index("seq"),
+        out_weight.shape[0],
+    )
+    sheets = tuple(((p, (p + 1) % finding) for p in range(finding)))
+    weight_piece = jnp.zeros(
+        (*out_weight.shape[:0], finding * view_out, *out_weight.shape[1:]), out_weight.dtype
+    )
+    k_now = out_weight
+    for i0 in range(finding):
+        r2 = (u1 - i0) % finding
+        weight_piece = lax.dynamic_update_slice_in_dim(weight_piece, k_now, r2 * view_out, axis=0)
+        if i0 < finding - 1:
+            k_now = jax.lax.ppermute(k_now, "seq", sheets)
     total_out = jnp.dot(gated_rows, weight_piece, preferred_element_type=jnp.float32)
     column = lax.dot_general(
         cotangent, weight_piece, (((1,), (1,)), ((), ())), preferred_element_type=jnp.float32

time: 416 us -> 518 us (1.25)
  waiting for transfers between devices: 256 us -> 328 us
  local copies, waits for them, and re-layouts: 49.7 us -> 84.4 us
  between operations: 15.2 us -> 2.18 us
  starting transfers between devices: 28 us -> 40.5 us
    ppermute x0 -> x15, waiting for transfers between devices: none -> 202 us  [on_device(): k_now = jax.lax.ppermute(k_now, 'seq', sheets)]
    all_to_all x2, waiting for transfers between devices: 110 us -> 41.5 us  [relay_pass(): lax.all_to_all(columns, 'seq', split_axis=0, concat_axis=1, tiled=True)]
    all_gather x1 -> x0, waiting for transfers between devices: 60 us -> none  [on_device(): weight_piece = lax.all_gather(out_weight, 'seq', axis=0, tiled=True)]
    dynamic_update_slice x0 -> x16, local copies, waits for them, and re-layouts: none -> 27.1 us  [on_device(): lax.dynamic_update_slice_in_dim(weight_piece, k_now, r2 * view_out, axis=0)]
    all_to_all x2, starting transfers between devices: 13.3 us -> 25.5 us  [relay_pass(): lax.all_to_all(columns, 'seq', split_axis=0, concat_axis=1, tiled=True)]
    broadcast_in_dim x0 -> x1, local copies, waits for them, and re-layouts: none -> 6.02 us  [on_device(): jnp.zeros((*out_weight.shape[:0], finding * view_out, *out_weight.shape[1...]
  transfers between devices with their start and end apart: 7 -> 21, of which waited for: 5 -> 17; matrix products, arithmetic and copies ran while one was open for 13% -> 16% of each run, Pallas kernels for 0% -> 0%
where the time goes in v1:
time: 518 us; the launch traced here: 516 us
  waiting for transfers between devices  328 us (63%)
  local copies, waits for them, and re-layouts  84.4 us (16%)
  starting transfers between devices  40.5 us (8%)
  other arithmetic  34.8 us (7%)
  matrix products  25.5 us (5%)
    ppermute x15, waiting for transfers between devices, on_device(): k_now = jax.lax.ppermute(k_now, 'seq', sheets)  202 us
    all_to_all x2, waiting for transfers between devices, relay_pass(): lax.all_to_all(result.reshape(share_width, block_count * BLOCK), 'seq', s...  85.3 us
    all_to_all x2, waiting for transfers between devices, relay_pass(): lax.all_to_all(columns, 'seq', split_axis=0, concat_axis=1, tiled=True)  41.5 us
    dynamic_update_slice x16, local copies, waits for them, and re-layouts, on_device(): lax.dynamic_update_slice_in_dim(weight_piece, k_now, r2 * view_out, axis=0)  27.1 us
    all_to_all x2, starting transfers between devices, relay_pass(): lax.all_to_all(columns, 'seq', split_axis=0, concat_axis=1, tiled=True)  25.5 us
    rev x2, local copies, waits for them, and re-layouts, relay_pass(): blocked = jnp.flip(blocked, axis=(1, 2))  18.4 us
    dot_general x1, matrix products, on_device(): jnp.dot(gated_rows, weight_piece, preferred_element_type=jnp.float32)  11.6 us
  transfers between devices with their start and end apart: 21, of which 17 were waited for; matrix products, arithmetic and copies ran while one was open for 16% of the time, Pallas kernels for 0%

profile of v1, /device:TPU:16, one launch (start us, length us, event | category | flops | bytes accessed | tf_op | source)
XLA Modules:
  0.0 515.7 jit_solution(15141145278257511311)
XLA Ops:
  0.7 15.3 %collective-permute-done.1 = bf16[128,4096]{1,0:T(8,128)(2,1)S(1)} collective-permute-done((bf16[128,4096]{1,0:T(8,128)(2,1)}, bf16[128,4096]{1,0:T(8,128)(2,1)S(1)}, u32[]{:S(2)}, u32[]{:S(2)}) %collective-permute-start.1) | collective-permute-done | bytes 1048608 | tf_op jit(solution)/shard_map/ppermute | solution.py:151
  17.0 14.2 %collective-permute-done.2 = bf16[128,4096]{1,0:T(8,128)(2,1)S(1)} collective-permute-done((bf16[128,4096]{1,0:T(8,128)(2,1)S(1)}, bf16[128,4096]{1,0:T(8,128)(2,1)S(1)}, u32[]{:S(2)}, u32[]{:S(2)}) %collective-permute-start.2) | collective-permute-done | bytes 1048608 | tf_op jit(solution)/shard_map/ppermute | solution.py:151
  31.2 15.1 %collective-permute-done.3 = bf16[128,4096]{1,0:T(8,128)(2,1)S(1)} collective-permute-done((bf16[128,4096]{1,0:T(8,128)(2,1)S(1)}, bf16[128,4096]{1,0:T(8,128)(2,1)S(1)}, u32[]{:S(2)}, u32[]{:S(2)}) %collective-permute-start.3) | collective-permute-done | bytes 1048608 | tf_op jit(solution)/shard_map/ppermute | solution.py:151
  47.3 15.2 %collective-permute-done.4 = bf16[128,4096]{1,0:T(8,128)(2,1)} collective-permute-done((bf16[128,4096]{1,0:T(8,128)(2,1)S(1)}, bf16[128,4096]{1,0:T(8,128)(2,1)}, u32[]{:S(2)}, u32[]{:S(2)}) %collective-permute-start.4) | collective-permute-done | bytes 1048608 | tf_op jit(solution)/shard_map/ppermute | solution.py:151
  64.1 1.9 collective-permute-start
  66.1 11.9 %collective-permute-done.5 = bf16[128,4096]{1,0:T(8,128)(2,1)} collective-permute-done((bf16[128,4096]{1,0:T(8,128)(2,1)}, bf16[128,4096]{1,0:T(8,128)(2,1)}, u32[]{:S(2)}, u32[]{:S(2)}) %collective-permute-start.5) | collective-permute-done | bytes 1048608 | tf_op jit(solution)/shard_map/ppermute | solution.py:151
  81.5 11.8 %collective-permute-done.6 = bf16[128,4096]{1,0:T(8,128)(2,1)} collective-permute-done((bf16[128,4096]{1,0:T(8,128)(2,1)}, bf16[128,4096]{1,0:T(8,128)(2,1)}, u32[]{:S(2)}, u32[]{:S(2)}) %collective-permute-start.6) | collective-permute-done | bytes 1048608 | tf_op jit(solution)/shard_map/ppermute | solution.py:151
  96.4 12.4 %collective-permute-done.7 = bf16[128,4096]{1,0:T(8,128)(2,1)} collective-permute-done((bf16[128,4096]{1,0:T(8,128)(2,1)}, bf16[128,4096]{1,0:T(8,128)(2,1)}, u32[]{:S(2)}, u32[]{:S(2)}) %collective-permute-start.7) | collective-permute-done | bytes 1048608 | tf_op jit(solution)/shard_map/ppermute | solution.py:151
  110.7 3.2 multiply_bitcast_fusion.1
  115.5 18.2 %all-to-all-start = ((f32[16,128,256]{1,2,0:T(8,128)}), f32[16,128,256]{1,2,0:T(8,128)}, u32[]{:S(2)}, u32[]{:S(2)}) async-start(f32[16,128,256]{1,2,0:T(8,128)} %bitcast.122), calls=%async_computation | async-start | bytes 4194304 | tf_op jit(solution)/shard_map/all_to_all | solution.py:59
  136.3 56.3 %collective-permute-done.9 = bf16[128,4096]{1,0:T(8,128)(2,1)S(1)} collective-permute-done((bf16[128,4096]{1,0:T(8,128)(2,1)}, bf16[128,4096]{1,0:T(8,128)(2,1)S(1)}, u32[]{:S(2)}, u32[]{:S(2)}) %collective-permute-start.9) | collective-permute-done | bytes 1048608 | tf_op jit(solution)/shard_map/ppermute | solution.py:151
  198.3 6.0 %broadcast_in_dim.2 = bf16[2048,4096]{1,0:T(8,128)(2,1)} broadcast(bf16[]{:T(256)} %constant.137.clone.1), dimensions={} | broadcast | bytes 16777218 | tf_op jit(solution)/shard_map/broadcast_in_dim | solution.py:143
  205.3 2.5 collective-permute-done.10
  211.8 11.5 %collective-permute-done.11 = bf16[128,4096]{1,0:T(8,128)(2,1)} collective-permute-done((bf16[128,4096]{1,0:T(8,128)(2,1)}, bf16[128,4096]{1,0:T(8,128)(2,1)}, u32[]{:S(2)}, u32[]{:S(2)}) %collective-permute-start.11) | collective-permute-done | bytes 1048608 | tf_op jit(solution)/shard_map/ppermute | solution.py:151
  224.3 2.9 copy.23
  227.2 2.3 constant_dynamic-update-slice_fusion.11
  229.5 2.3 constant_dynamic-update-slice_fusion.10
  231.9 6.8 %collective-permute-done.12 = bf16[128,4096]{1,0:T(8,128)(2,1)} collective-permute-done((bf16[128,4096]{1,0:T(8,128)(2,1)}, bf16[128,4096]{1,0:T(8,128)(2,1)}, u32[]{:S(2)}, u32[]{:S(2)}) %collective-permute-start.12) | collective-permute-done | bytes 1048608 | tf_op jit(solution)/shard_map/ppermute | solution.py:151
  238.7 2.4 constant_dynamic-update-slice_fusion.9
  241.1 2.3 constant_dynamic-update-slice_fusion.8
  243.4 2.3 constant_dynamic-update-slice_fusion.7
  245.7 8.3 %collective-permute-done.13 = bf16[128,4096]{1,0:T(8,128)(2,1)S(1)} collective-permute-done((bf16[128,4096]{1,0:T(8,128)(2,1)}, bf16[128,4096]{1,0:T(8,128)(2,1)S(1)}, u32[]{:S(2)}, u32[]{:S(2)}) %collective-permute-start.13) | collective-permute-done | bytes 1048608 | tf_op jit(solution)/shard_map/ppermute | solution.py:151
  255.1 2.3 constant_dynamic-update-slice_fusion.5
  257.4 2.3 constant_dynamic-update-slice_fusion.4
  259.7 9.4 %collective-permute-done.14 = bf16[128,4096]{1,0:T(8,128)(2,1)S(1)} collective-permute-done((bf16[128,4096]{1,0:T(8,128)(2,1)S(1)}, bf16[128,4096]{1,0:T(8,128)(2,1)S(1)}, u32[]{:S(2)}, u32[]{:S(2)}) %collective-permute-start.14) | collective-permute-done | bytes 1048608 | tf_op jit(solution)/shard_map/ppermute | solution.py:151
  269.1 2.3 constant_dynamic-update-slice_fusion.3
  273.5 10.8 %collective-permute-done.15 = bf16[128,4096]{1,0:T(8,128)(2,1)S(1)} collective-permute-done((bf16[128,4096]{1,0:T(8,128)(2,1)S(1)}, bf16[128,4096]{1,0:T(8,128)(2,1)S(1)}, u32[]{:S(2)}, u32[]{:S(2)}) %collective-permute-start.15) | collective-permute-done | bytes 1048608 | tf_op jit(solution)/shard_map/ppermute | solution.py:151
  285.4 8.3 %convolution_bitcast_fusion = f32[256,2048]{1,0:T(8,128)S(1)} fusion(bf16[2048,4096]{1,0:T(8,128)(2,1)} %constant_dynamic-update-slice_fusion, bf16[256,4096]{1,0:T(8,128)(2,1)S(1)} %copy-done), kind=kOutput, calls=%fused_computation.7 | convolution fusion | flops 4294967296 | bytes 20971520 | tf_op jit(solution)/shard_map/dot_general | solution.py:153
  293.7 2.2 multiply_bitcast_fusion
  297.5 7.4 %all-to-all-start.2 = ((f32[16,128,256]{1,2,0:T(8,128)}), f32[16,128,256]{1,2,0:T(8,128)}, u32[]{:S(2)}, u32[]{:S(2)}) async-start(f32[16,128,256]{1,2,0:T(8,128)} %bitcast.123), calls=%async_computation.2 | async-start | bytes 4194304 | tf_op jit(solution)/shard_map/all_to_all | solution.py:59
  304.9 2.8 fusion.4
  307.8 2.0 copy-done.5
  311.1 41.5 %all-to-all-done.2 = f32[16,128,256]{1,2,0:T(8,128)} async-done(((f32[16,128,256]{1,2,0:T(8,128)}), f32[16,128,256]{1,2,0:T(8,128)}, u32[]{:S(2)}, u32[]{:S(2)}) %all-to-all-start.2) | async-done | bytes 2097184 | tf_op jit(solution)/shard_map/all_to_all | solution.py:59
  352.6 16.5 %rev.11 = f32[128,32,128]{0,2,1:T(8,128)} reverse(f32[128,32,128]{0,2,1:T(8,128)} %bitcast.33), dimensions={1,2} | reverse | bytes 4194304 | tf_op jit(solution)/shard_map/jit(_flip)/rev | solution.py:70
  369.2 1.9 copy.27
  371.1 2.8 fusion.7
  374.0 1.9 copy-done.6
  377.3 6.8 %multiply_reduce_fusion = (f32[128,32,128]{0,2,1:T(8,128)S(1)}, f32[128,32,128]{0,2,1:T(8,128)}) fusion(f32[2,128,32,128]{1,3,2,0:T(8,128)} %copy-done.6, f32[2,128,32]{1,2,0:T(8,128)S(1)} %pad_multiply_fusion, f32[2,128]{1,0:T(2,128)S(1)} %copy-done.42, f32[2,128,128]{1,2,0:T(8,128)S(1)} %get-tuple-element.90, f32[2,128,32,128]{1,3,2,0:T(8,128)} %copy-done.5, ...), kind=kLoop, calls=%fused_computation.1 | loop fusion | flops 7340032 | bytes 12780544 | tf_op jit(solution)/shard_map/reduce_sum | solution.py:54
  384.0 4.7 all-to-all-start.1
  388.7 10.1 %rev.13 = f32[128,32,128]{0,2,1:T(8,128)} reverse(f32[128,32,128]{0,2,1:T(8,128)S(1)} %get-tuple-element.4), dimensions={1,2} | reverse | bytes 4194304 | tf_op jit(solution)/shard_map/jit(_flip)/rev | solution.py:78
  398.9 37.6 %all-to-all-done.1 = f32[128,16,256]{0,2,1:T(8,128)} async-done(((f32[128,16,256]{0,2,1:T(8,128)}), f32[128,16,256]{0,2,1:T(8,128)}, u32[]{:S(2)}, u32[]{:S(2)}) %all-to-all-start.1) | async-done | bytes 2097184 | tf_op jit(solution)/shard_map/all_to_all | solution.py:79
  436.5 4.8 all-to-all-start.3
  441.4 47.7 %all-to-all-done.3 = f32[128,16,256]{0,2,1:T(8,128)} async-done(((f32[128,16,256]{0,2,1:T(8,128)}), f32[128,16,256]{0,2,1:T(8,128)}, u32[]{:S(2)}, u32[]{:S(2)}) %all-to-all-start.3) | async-done | bytes 2097184 | tf_op jit(solution)/shard_map/all_to_all | solution.py:79
  489.0 5.2 %fusion.65 = (f32[256,2048]{1,0:T(8,128)S(1)}, f32[256,2048]{1,0:T(8,128)S(1)}, f32[256,2048]{1,0:T(8,128)S(1)}, f32[256,2048]{1,0:T(8,128)S(1)}) fusion(f32[256,2048]{1,0:T(8,128)} %get-tuple-element.13, f32[256,2048]{1,0:T(8,128)} %copy-done.8, f32[256,2048]{1,0:T(8,128)} %get-tuple-element.18, f32[2048]{0:T(1024)S(1)} %copy-done.40, ...), kind=kLoop, calls=%fused_computation.207 | loop fusion | flops 4194304 | bytes 20979712 | tf_op jit(solution)/shard_map/mul | solution.py:164
  494.7 3.2 collective-permute-start.16
  497.9 11.6 %convolution_convert_fusion = bf16[256,4096]{1,0:T(8,128)(2,1)} fusion(bf16[2048,4096]{1,0:T(8,128)(2,1)} %constant_dynamic-update-slice_fusion, f32[256,2048]{1,0:T(8,128)S(1)} %copy-done.7, f32[256,2048]{1,0:T(8,128)S(1)} %get-tuple-element.20), kind=kOutput, calls=%fused_computation | convolution fusion | flops 4297064448 | bytes 23068672 | tf_op jit(solution)/shard_map/dot_general | solution.py:152
  509.6 1.9 fusion.24
  511.5 4.2 fusion.14
  (309 shorter events, 36.0 us)
Async XLA Ops:
  0.6 284.7 %copy-start = (bf16[256,4096]{1,0:T(8,128)(2,1)S(1)}, bf16[256,4096]{1,0:T(8,128)(2,1)}, u32[]{:S(2)}) copy-start(bf16[256,4096]{1,0:T(8,128)(2,1)} %param.18) | copy-start | bytes 6291460
  0.6 109.7 %copy-start.9 = (bf16[256,2048]{1,0:T(8,128)(2,1)S(1)}, bf16[256,2048]{1,0:T(8,128)(2,1)}, u32[]{:S(2)}) copy-start(bf16[256,2048]{1,0:T(8,128)(2,1)} %param.11) | copy-start | bytes 3145732
  0.7 15.4 %collective-permute-start.1 = (bf16[128,4096]{1,0:T(8,128)(2,1)}, bf16[128,4096]{1,0:T(8,128)(2,1)S(1)}, u32[]{:S(2)}, u32[]{:S(2)}) collective-permute-start(bf16[128,4096]{1,0:T(8,128)(2,1)} %param.17), channel_id=1, source_target_pairs={{0,1},{1,2},{2,3},{3,4},{4,5},{5,6},{6,7},{7,8},{8,9},{9,10},{10,1... | collective-permute-start | bytes 3145736 | tf_op jit(solution)/shard_map/ppermute | solution.py:151
  16.0 15.1 %collective-permute-start.2 = (bf16[128,4096]{1,0:T(8,128)(2,1)S(1)}, bf16[128,4096]{1,0:T(8,128)(2,1)S(1)}, u32[]{:S(2)}, u32[]{:S(2)}) collective-permute-start(bf16[128,4096]{1,0:T(8,128)(2,1)S(1)} %collective-permute-done.1), channel_id=1, source_target_pairs={{0,1},{1,2},{2,3},{3,4},{4,5},{5,6},{6,7},{7,8},{8,9},{9,10},{10,1... | collective-permute-start | bytes 3145736 | tf_op jit(solution)/shard_map/ppermute | solution.py:151
  31.2 31.3 %copy-start.16 = (bf16[128,4096]{1,0:T(8,128)(2,1)}, bf16[128,4096]{1,0:T(8,128)(2,1)S(1)}, u32[]{:S(2)}) copy-start(bf16[128,4096]{1,0:T(8,128)(2,1)S(1)} %collective-permute-done.2) | copy-start | bytes 3145732
  31.2 15.1 %collective-permute-start.3 = (bf16[128,4096]{1,0:T(8,128)(2,1)S(1)}, bf16[128,4096]{1,0:T(8,128)(2,1)S(1)}, u32[]{:S(2)}, u32[]{:S(2)}) collective-permute-start(bf16[128,4096]{1,0:T(8,128)(2,1)S(1)} %collective-permute-done.2), channel_id=1, source_target_pairs={{0,1},{1,2},{2,3},{3,4},{4,5},{5,6},{6,7},{7,8},{8,9},{9,10},{10,1... | collective-permute-start | bytes 3145736 | tf_op jit(solution)/shard_map/ppermute | solution.py:151
  47.3 15.2 %collective-permute-start.4 = (bf16[128,4096]{1,0:T(8,128)(2,1)S(1)}, bf16[128,4096]{1,0:T(8,128)(2,1)}, u32[]{:S(2)}, u32[]{:S(2)}) collective-permute-start(bf16[128,4096]{1,0:T(8,128)(2,1)S(1)} %collective-permute-done.3), channel_id=1, source_target_pairs={{0,1},{1,2},{2,3},{3,4},{4,5},{5,6},{6,7},{7,8},{8,9},{9,10},{10,1... | collective-permute-start | bytes 3145736 | tf_op jit(solution)/shard_map/ppermute | solution.py:151
  62.5 15.4 %collective-permute-start.5 = (bf16[128,4096]{1,0:T(8,128)(2,1)}, bf16[128,4096]{1,0:T(8,128)(2,1)}, u32[]{:S(2)}, u32[]{:S(2)}) collective-permute-start(bf16[128,4096]{1,0:T(8,128)(2,1)} %collective-permute-done.4), channel_id=1, source_target_pairs={{0,1},{1,2},{2,3},{3,4},{4,5},{5,6},{6,7},{7,8},{8,9},{9,10},{10,1... | collective-permute-start | bytes 3145736 | tf_op jit(solution)/shard_map/ppermute | solution.py:151
  64.1 31.7 %collective-permute-start = (bf16[3,2,2048]{2,1,0:T(2,128)(2,1)S(1)}, bf16[3,2,2048]{2,1,0:T(2,128)(2,1)S(1)}, u32[]{:S(2)}, u32[]{:S(2)}) collective-permute-start(bf16[3,2,2048]{2,1,0:T(2,128)(2,1)S(1)} %pad_maximum_fusion.3), channel_id=1, source_target_pairs={{0,1},{1,2},{2,3},{3,4},{4,5},{5,6},{6,7},{7,8},{8,9},{9,10},{10,1... | collective-permute-start | bytes 73736 | tf_op jit(solution)/shard_map/ppermute | solution.py:13
  77.9 15.4 %collective-permute-start.6 = (bf16[128,4096]{1,0:T(8,128)(2,1)}, bf16[128,4096]{1,0:T(8,128)(2,1)}, u32[]{:S(2)}, u32[]{:S(2)}) collective-permute-start(bf16[128,4096]{1,0:T(8,128)(2,1)} %collective-permute-done.5), channel_id=1, source_target_pairs={{0,1},{1,2},{2,3},{3,4},{4,5},{5,6},{6,7},{7,8},{8,9},{9,10},{10,1... | collective-permute-start | bytes 3145736 | tf_op jit(solution)/shard_map/ppermute | solution.py:151
  93.4 15.4 %collective-permute-start.7 = (bf16[128,4096]{1,0:T(8,128)(2,1)}, bf16[128,4096]{1,0:T(8,128)(2,1)}, u32[]{:S(2)}, u32[]{:S(2)}) collective-permute-start(bf16[128,4096]{1,0:T(8,128)(2,1)} %collective-permute-done.6), channel_id=1, source_target_pairs={{0,1},{1,2},{2,3},{3,4},{4,5},{5,6},{6,7},{7,8},{8,9},{9,10},{10,1... | collective-permute-start | bytes 3145736 | tf_op jit(solution)/shard_map/ppermute | solution.py:151
  93.5 17.2 %copy-start.36 = (f32[256]{0:T(256)}, f32[256]{0:T(256)S(1)}, u32[]{:S(2)}) copy-start(f32[256]{0:T(256)S(1)} %get-tuple-element.84) | copy-start | bytes 3076
  93.5 17.2 %copy-start.38 = (f32[256]{0:T(256)}, f32[256]{0:T(256)S(1)}, u32[]{:S(2)}) copy-start(f32[256]{0:T(256)S(1)} %get-tuple-element.85) | copy-start | bytes 3076
  95.1 15.6 %copy-start.18 = (f32[1,1,2048]{2,1,0:T(1,128)}, f32[1,1,2048]{2,1,0:T(1,128)S(1)}, u32[]{:S(2)}) copy-start(f32[1,1,2048]{2,1,0:T(1,128)S(1)} %get-tuple-element.23) | copy-start | bytes 24580
  95.1 15.6 %copy-start.20 = (f32[1,1,2048]{2,1,0:T(1,128)}, f32[1,1,2048]{2,1,0:T(1,128)S(1)}, u32[]{:S(2)}) copy-start(f32[1,1,2048]{2,1,0:T(1,128)S(1)} %get-tuple-element.24) | copy-start | bytes 24580
  95.1 15.6 %copy-start.22 = (f32[1,1,2048]{2,1,0:T(1,128)}, f32[1,1,2048]{2,1,0:T(1,128)S(1)}, u32[]{:S(2)}) copy-start(f32[1,1,2048]{2,1,0:T(1,128)S(1)} %get-tuple-element.28) | copy-start | bytes 24580
  95.1 15.6 %copy-start.24 = (f32[1,1,2048]{2,1,0:T(1,128)}, f32[1,1,2048]{2,1,0:T(1,128)S(1)}, u32[]{:S(2)}) copy-start(f32[1,1,2048]{2,1,0:T(1,128)S(1)} %get-tuple-element.29) | copy-start | bytes 24580
  108.8 24.8 %collective-permute-start.8 = (bf16[128,4096]{1,0:T(8,128)(2,1)}, bf16[128,4096]{1,0:T(8,128)(2,1)}, u32[]{:S(2)}, u32[]{:S(2)}) collective-permute-start(bf16[128,4096]{1,0:T(8,128)(2,1)} %collective-permute-done.7), channel_id=1, source_target_pairs={{0,1},{1,2},{2,3},{3,4},{4,5},{5,6},{6,7},{7,8},{8,9},{9,10},{10,1... | collective-permute-start | bytes 3145736 | tf_op jit(solution)/shard_map/ppermute | solution.py:151
  115.5 108.8 %all-to-all-start = ((f32[16,128,256]{1,2,0:T(8,128)}), f32[16,128,256]{1,2,0:T(8,128)}, u32[]{:S(2)}, u32[]{:S(2)}) async-start(f32[16,128,256]{1,2,0:T(8,128)} %bitcast.122), calls=%async_computation | async-start | bytes 4194304 | tf_op jit(solution)/shard_map/all_to_all | solution.py:59
  133.7 58.9 %collective-permute-start.9 = (bf16[128,4096]{1,0:T(8,128)(2,1)}, bf16[128,4096]{1,0:T(8,128)(2,1)S(1)}, u32[]{:S(2)}, u32[]{:S(2)}) collective-permute-start(bf16[128,4096]{1,0:T(8,128)(2,1)} %collective-permute-done.8), channel_id=1, source_target_pairs={{0,1},{1,2},{2,3},{3,4},{4,5},{5,6},{6,7},{7,8},{8,9},{9,10},{10,1... | collective-permute-start | bytes 3145736 | tf_op jit(solution)/shard_map/ppermute | solution.py:151
  135.6 61.8 %copy-start.47 = (f32[32]{0:T(128)}, f32[32]{0:T(128)S(1)}, u32[]{:S(2)}) copy-start(f32[32]{0:T(128)S(1)} %convert_subtract_fusion) | copy-start | bytes 388
  135.6 61.8 %copy-start.45 = (f32[32]{0:T(128)}, f32[32]{0:T(128)S(1)}, u32[]{:S(2)}) copy-start(f32[32]{0:T(128)S(1)} %broadcast_subtract_fusion.1) | copy-start | bytes 388
  192.6 15.2 %collective-permute-start.10 = (bf16[128,4096]{1,0:T(8,128)(2,1)S(1)}, bf16[128,4096]{1,0:T(8,128)(2,1)}, u32[]{:S(2)}, u32[]{:S(2)}) collective-permute-start(bf16[128,4096]{1,0:T(8,128)(2,1)S(1)} %collective-permute-done.9), channel_id=1, source_target_pairs={{0,1},{1,2},{2,3},{3,4},{4,5},{5,6},{6,7},{7,8},{8,9},{9,10},{10,1... | collective-permute-start | bytes 3145736 | tf_op jit(solution)/shard_map/ppermute | solution.py:151
  198.2 6.0 %copy-start.11 = (bf16[128,4096]{1,0:T(8,128)(2,1)S(1)}, bf16[128,4096]{1,0:T(8,128)(2,1)}, u32[]{:S(2)}) copy-start(bf16[128,4096]{1,0:T(8,128)(2,1)} %param.17) | copy-start | bytes 3145732
  207.8 15.4 %collective-permute-start.11 = (bf16[128,4096]{1,0:T(8,128)(2,1)}, bf16[128,4096]{1,0:T(8,128)(2,1)}, u32[]{:S(2)}, u32[]{:S(2)}) collective-permute-start(bf16[128,4096]{1,0:T(8,128)(2,1)} %collective-permute-done.10), channel_id=1, source_target_pairs={{0,1},{1,2},{2,3},{3,4},{4,5},{5,6},{6,7},{7,8},{8,9},{9,10},{10,1... | collective-permute-start | bytes 3145736 | tf_op jit(solution)/shard_map/ppermute | solution.py:151
  209.6 13.7 %copy-start.13 = (bf16[128,4096]{1,0:T(8,128)(2,1)S(1)}, bf16[128,4096]{1,0:T(8,128)(2,1)}, u32[]{:S(2)}) copy-start(bf16[128,4096]{1,0:T(8,128)(2,1)} %copy-done.12) | copy-start | bytes 3145732
  223.2 15.4 %collective-permute-start.12 = (bf16[128,4096]{1,0:T(8,128)(2,1)}, bf16[128,4096]{1,0:T(8,128)(2,1)}, u32[]{:S(2)}, u32[]{:S(2)}) collective-permute-start(bf16[128,4096]{1,0:T(8,128)(2,1)} %collective-permute-done.11), channel_id=1, source_target_pairs={{0,1},{1,2},{2,3},{3,4},{4,5},{5,6},{6,7},{7,8},{8,9},{9,10},{10,1... | collective-permute-start | bytes 3145736 | tf_op jit(solution)/shard_map/ppermute | solution.py:151
  238.7 15.3 %collective-permute-start.13 = (bf16[128,4096]{1,0:T(8,128)(2,1)}, bf16[128,4096]{1,0:T(8,128)(2,1)S(1)}, u32[]{:S(2)}, u32[]{:S(2)}) collective-permute-start(bf16[128,4096]{1,0:T(8,128)(2,1)} %collective-permute-done.12), channel_id=1, source_target_pairs={{0,1},{1,2},{2,3},{3,4},{4,5},{5,6},{6,7},{7,8},{8,9},{9,10},{10,1... | collective-permute-start | bytes 3145736 | tf_op jit(solution)/shard_map/ppermute | solution.py:151
  254.0 15.1 %collective-permute-start.14 = (bf16[128,4096]{1,0:T(8,128)(2,1)S(1)}, bf16[128,4096]{1,0:T(8,128)(2,1)S(1)}, u32[]{:S(2)}, u32[]{:S(2)}) collective-permute-start(bf16[128,4096]{1,0:T(8,128)(2,1)S(1)} %collective-permute-done.13), channel_id=1, source_target_pairs={{0,1},{1,2},{2,3},{3,4},{4,5},{5,6},{6,7},{7,8},{8,9},{9,10},{10,1... | collective-permute-start | bytes 3145736 | tf_op jit(solution)/shard_map/ppermute | solution.py:151
  269.1 15.1 %collective-permute-start.15 = (bf16[128,4096]{1,0:T(8,128)(2,1)S(1)}, bf16[128,4096]{1,0:T(8,128)(2,1)S(1)}, u32[]{:S(2)}, u32[]{:S(2)}) collective-permute-start(bf16[128,4096]{1,0:T(8,128)(2,1)S(1)} %collective-permute-done.14), channel_id=1, source_target_pairs={{0,1},{1,2},{2,3},{3,4},{4,5},{5,6},{6,7},{7,8},{8,9},{9,10},{10,1... | collective-permute-start | bytes 3145736 | tf_op jit(solution)/shard_map/ppermute | solution.py:151
  285.3 8.4 %copy-start.2 = (f32[258,2048]{1,0:T(8,128)S(1)}, f32[258,2048]{1,0:T(8,128)}, u32[]{:S(2)}) copy-start(f32[258,2048]{1,0:T(8,128)} %maximum_convert_fusion) | copy-start | bytes 6340612
  285.3 8.4 %copy-start.26 = (f32[1,1,2048]{2,1,0:T(1,128)S(1)}, f32[1,1,2048]{2,1,0:T(1,128)}, u32[]{:S(2)}) copy-start(f32[1,1,2048]{2,1,0:T(1,128)} %get-tuple-element.25) | copy-start | bytes 24580
  285.3 8.4 %copy-start.27 = (f32[1,1,2048]{2,1,0:T(1,128)S(1)}, f32[1,1,2048]{2,1,0:T(1,128)}, u32[]{:S(2)}) copy-start(f32[1,1,2048]{2,1,0:T(1,128)} %get-tuple-element.26) | copy-start | bytes 24580
  285.3 8.4 %copy-start.28 = (f32[1,1,2048]{2,1,0:T(1,128)S(1)}, f32[1,1,2048]{2,1,0:T(1,128)}, u32[]{:S(2)}) copy-start(f32[1,1,2048]{2,1,0:T(1,128)} %get-tuple-element.27) | copy-start | bytes 24580
  285.3 8.4 %copy-start.37 = (f32[256]{0:T(256)S(1)}, f32[256]{0:T(256)}, u32[]{:S(2)}) copy-start(f32[256]{0:T(256)} %copy-done.36) | copy-start | bytes 3076
  285.4 8.4 %copy-start.39 = (f32[256]{0:T(256)S(1)}, f32[256]{0:T(256)}, u32[]{:S(2)}) copy-start(f32[256]{0:T(256)} %copy-done.38) | copy-start | bytes 3076
  297.5 7.4 %copy-start.3 = (f32[128,32,128]{2,0,1:T(8,128)S(1)}, f32[128,32,128]{2,0,1:T(8,128)}, u32[]{:S(2)}) copy-start(f32[128,32,128]{2,0,1:T(8,128)} %copy.23) | copy-start | bytes 6291460
  297.5 55.1 %all-to-all-start.2 = ((f32[16,128,256]{1,2,0:T(8,128)}), f32[16,128,256]{1,2,0:T(8,128)}, u32[]{:S(2)}, u32[]{:S(2)}) async-start(f32[16,128,256]{1,2,0:T(8,128)} %bitcast.123), calls=%async_computation.2 | async-start | bytes 4194304 | tf_op jit(solution)/shard_map/all_to_all | solution.py:59
  304.9 6.0 %copy-start.44 = (f32[2,128,1]{1,2,0:T(1,128)S(1)}, f32[2,128,1]{1,2,0:T(1,128)}, u32[]{:S(2)}) copy-start(f32[2,128,1]{1,2,0:T(1,128)} %slice.607) | copy-start | bytes 3076
  304.9 6.1 %copy-start.48 = (f32[32]{0:T(128)S(1)}, f32[32]{0:T(128)}, u32[]{:S(2)}) copy-start(f32[32]{0:T(128)} %copy-done.47) | copy-start | bytes 388
  371.1 5.9 %copy-start.43 = (f32[2,128,1]{1,2,0:T(1,128)S(1)}, f32[2,128,1]{1,2,0:T(1,128)}, u32[]{:S(2)}) copy-start(f32[2,128,1]{1,2,0:T(1,128)} %slice.639) | copy-start | bytes 3076
  371.1 6.1 %copy-start.46 = (f32[32]{0:T(128)S(1)}, f32[32]{0:T(128)}, u32[]{:S(2)}) copy-start(f32[32]{0:T(128)} %copy-done.45) | copy-start | bytes 388
  371.1 6.1 %copy-start.42 = (f32[2,128]{1,0:T(2,128)S(1)}, f32[2,128]{1,0:T(2,128)}, u32[]{:S(2)}) copy-start(f32[2,128]{1,0:T(2,128)} %get-tuple-element.15) | copy-start | bytes 3076
  384.0 52.4 %all-to-all-start.1 = ((f32[128,16,256]{0,2,1:T(8,128)}), f32[128,16,256]{0,2,1:T(8,128)}, u32[]{:S(2)}, u32[]{:S(2)}) async-start(f32[128,16,256]{0,2,1:T(8,128)} %bitcast.121), calls=%async_computation.1 | async-start | bytes 4194304 | tf_op jit(solution)/shard_map/all_to_all | solution.py:79
  436.5 52.6 %copy-start.4 = (f32[256,2048]{1,0:T(8,128)S(1)}, f32[256,2048]{1,0:T(8,128)}, u32[]{:S(2)}) copy-start(f32[256,2048]{1,0:T(8,128)} %get-tuple-element.14) | copy-start | bytes 6291460
  436.5 52.6 %copy-start.40 = (f32[2048]{0:T(1024)S(1)}, f32[2048]{0:T(1024)}, u32[]{:S(2)}) copy-start(f32[2048]{0:T(1024)} %param.16) | copy-start | bytes 24580
  436.5 52.6 %all-to-all-start.3 = ((f32[128,16,256]{0,2,1:T(8,128)}), f32[128,16,256]{0,2,1:T(8,128)}, u32[]{:S(2)}, u32[]{:S(2)}) async-start(f32[128,16,256]{0,2,1:T(8,128)} %bitcast.124), calls=%async_computation.3 | async-start | bytes 4194304 | tf_op jit(solution)/shard_map/all_to_all | solution.py:79
  494.7 14.8 %collective-permute-start.16 = (bf16[3,2,2048]{2,1,0:T(2,128)(2,1)S(1)}, bf16[3,2,2048]{2,1,0:T(2,128)(2,1)S(1)}, u32[]{:S(2)}, u32[]{:S(2)}) collective-permute-start(bf16[3,2,2048]{2,1,0:T(2,128)(2,1)S(1)} %pad_maximum_fusion.4), channel_id=1, source_target_pairs={{1,0},{2,1},{3,2},{4,3},{5,4},{6,5},{7,6},{8,7},{9,8},{10,9},{11,1... | collective-permute-start | bytes 73736 | tf_op jit(solution)/shard_map/ppermute | solution.py:13
  (22 other events, 74.3 us)
